TPU v7x, 512 devices: a whole 4x4x16 slice. The times are simulated.
512 devices in a mesh: dp: 32 (over x, z_hi, core), tensor: 16 (over y, z_lo).
Axes of the slice: x: 4, y: 4, z: 16 (z_hi: 4, z_lo: 4; z = z_hi * 4 + z_lo), core: 2. Of those that a mesh axis runs over, the one named last changes fastest.
Arguments:
- tokens: bfloat16 [4096, 4096], P('dp', 'tensor'), may hold values from -6 to 6
- weight: bfloat16 [4096, 14336], P('dp', 'tensor'), may hold values from -0.09375 to 0.09375
- cotangent: bfloat16 [4096, 14336], P('dp', 'tensor'), may hold values from -6 to 6
- levels: int32 [28], replicated, may hold values from 0 to 8
Outputs:
- output: bfloat16 [4096, 14336], P('dp', 'tensor')
- input_grad: bfloat16 [4096, 4096], P('dp', 'tensor')
- weight_grad: float32 [4096, 14336], P('dp', 'tensor')
All inputs are finite; a program needn't handle non-finite values.
Results may differ from a plain program's by a relative error of at most 0.022.
Values may be sent and summed in bfloat16 or wider, within the bound.
No kernel may reach another device: no remote copies, remote signals or barrier semaphores. Data moves between devices by JAX's collectives and lax.ppermute only.
A program may use at most 128 MiB of HBM per device.

v0:
```python
import jax
import jax.numpy as jnp
from jax import lax
from jax.sharding import PartitionSpec as P

BLOCK = 512


def on_device(tokens, weight, cotangent, levels):
    token_rows = tokens.shape[0]
    local_cols = weight.shape[1]
    dp_count = lax.axis_size("dp")
    col_start = lax.axis_index("tensor") * local_cols
    column_ids = col_start + jnp.arange(local_cols, dtype=jnp.int32)
    block_ids = column_ids // BLOCK
    block_range = jnp.arange(levels.shape[0], dtype=jnp.int32)
    membership = (block_ids[None, :] == block_range[:, None]).astype(jnp.float32)
    level_vals = levels.astype(jnp.float32) / 8.0
    col_scale = jnp.sum(membership * level_vals[:, None], axis=0)
    features_all = lax.all_gather(tokens, "tensor", axis=1, tiled=True)
    scaled = (cotangent.astype(jnp.float32) * col_scale[None, :]).astype(jnp.bfloat16)
    transpose_dims = (((1,), (1,)), ((), ()))
    weight_piece = lax.all_gather(weight, "dp", axis=0, tiled=True)
    running = jnp.dot(features_all, weight_piece, preferred_element_type=jnp.float32)
    input_term = lax.dot_general(
        scaled, weight_piece, transpose_dims, preferred_element_type=jnp.float32
    )
    output = (running * col_scale[None, :]).astype(jnp.bfloat16)
    input_grad = lax.psum_scatter(
        input_term.astype(jnp.bfloat16), "tensor", scatter_dimension=1, tiled=True
    )
    grad_factor = 1.0 / jnp.sqrt(jnp.float32(token_rows * dp_count))
    local_grad = lax.dot_general(
        features_all, scaled, (((0,), (0,)), ((), ())), preferred_element_type=jnp.float32
    ).astype(jnp.bfloat16)
    grad_blocks = lax.all_to_all(local_grad[None], "dp", split_axis=1, concat_axis=0, tiled=True)
    weight_grad = jnp.sum(grad_blocks.astype(jnp.float32), axis=0) * grad_factor
    return (output, input_grad, weight_grad)


def solution(mesh):
    placed = (P("dp", "tensor"), P("dp", "tensor"), P("dp", "tensor"), P())
    return jax.shard_map(
        on_device,
        mesh=mesh,
        in_specs=placed,
        out_specs=(P("dp", "tensor"), P("dp", "tensor"), P("dp", "tensor")),
        check_vma=False,
    )
```

profile of v0, /device:TPU:6, one launch (start us, length us, event | category | flops | bytes accessed | tf_op | source)
XLA Modules:
  0.0 842.1 jit_solution(6824035741599947673)
XLA Ops:
  8.0 0.0 all-gather.3.cloned.1.call-start
  8.0 0.7 all-gather.3.cloned.1.call-update
  8.8 0.7 convert_multiply_fusion
  9.4 0.1 select_reduce_fusion
  9.5 82.2 %all-gather.3.cloned.1.call-done = bf16[128,4096]{1,0:T(8,128)(2,1)} async-done(((bf16[128,256]{1,0:T(8,128)(2,1)}), bf16[128,4096]{1,0:T(8,128)(2,1)}) %all-gather.3.cloned.1.call-update) | async-done | bytes 1048592 | tf_op jit(solution)/shard_map/all_gather | solution.py:20
  91.7 6.4 convert_bitcast_fusion
  98.1 32.2 %copy.10 = bf16[1,4096,896]{2,0,1:T(2,128)(2,1)} copy(bf16[1,4096,896]{1,2,0:T(8,128)(2,1)} %convert_bitcast_fusion) | data formatting | bytes 14680064 | tf_op jit(solution)/shard_map/broadcast_in_dim | solution.py:36
  130.3 0.5 broadcast.51
  130.8 157.1 %reduce = bf16[4096,896]{1,0:T(8,128)(2,1)} reduce(bf16[4096,1,896]{2,1,0:T(2,128)(2,1)} %bitcast.12, bf16[]{:T(256)} %broadcast.51), dimensions={1}, to_apply=%bitcast.5.reduce_sub_computation | reduce | bytes 14680066
  287.9 19.5 %reshape.33 = bf16[32,2,57344]{2,1,0:T(2,128)(2,1)} reshape(bf16[4096,896]{1,0:T(8,128)(2,1)} %reduce) | data formatting | bytes 14680064
  307.4 0.0 copy-start.1
  307.4 13.1 %all-to-all-start = ((bf16[32,2,57344]{2,1,0:T(2,128)(2,1)}), bf16[32,2,57344]{2,1,0:T(2,128)(2,1)}, u32[]{:S(2)}, u32[]{:S(2)}) async-start(bf16[32,2,57344]{2,1,0:T(2,128)(2,1)} %reshape.33), calls=%async_computation.1 | async-start | bytes 14680064 | tf_op jit(solution)/shard_map/all_to_all | solution.py:36
  320.4 0.0 copy-start
  320.4 0.0 all-gather.5.cloned.1.call-start
  320.5 0.5 all-gather.5.cloned.1.call-update
  321.0 0.2 reduce-scatter.2.cloned.1.call-start
  321.3 418.9 %all-gather.5.cloned.1.call-done = bf16[4096,896]{1,0:T(8,128)(2,1)} async-done(((bf16[128,896]{1,0:T(8,128)(2,1)}), bf16[4096,896]{1,0:T(8,128)(2,1)}) %all-gather.5.cloned.1.call-update) | async-done | bytes 7340048 | tf_op jit(solution)/shard_map/all_gather | solution.py:23
  740.2 0.0 copy-done.1
  740.2 6.6 convolution_convert_fusion
  746.8 0.0 reduce-scatter.2.cloned.1.call-update
  746.8 0.0 copy-done
  746.8 5.0 fusion
  751.8 0.0 all-to-all-done
  751.8 22.7 %reshape.34 = bf16[4096,1,896]{2,1,0:T(2,128)(2,1)} reshape(bf16[32,2,57344]{2,1,0:T(2,128)(2,1)} %all-to-all-done) | data formatting | bytes 14680064
  774.5 11.3 %copy.13 = f32[1,4096,896]{2,1,0:T(8,128)} copy(bf16[1,4096,896]{2,0,1:T(2,128)(2,1)} %bitcast.13) | data formatting | bytes 22020096
  785.9 5.9 reduce_sum.19
  791.8 0.2 copy.14
  792.0 1.0 copy.12
  793.0 41.6 %reduce-scatter.2.cloned.1.call-done = bf16[128,256]{1,0:T(8,128)(2,1)} async-done(((bf16[128,4096]{1,0:T(8,128)(2,1)}), bf16[128,256]{1,0:T(8,128)(2,1)}) %reduce-scatter.2.cloned.1.call-update) | async-done | bytes 65552 | tf_op jit(solution)/shard_map/reduce_scatter | solution.py:29
  (2 shorter events, 0.0 us)
Async XLA Ops:
  8.0 83.7 %all-gather.3.cloned.1.call-start = ((), (), s32[]{:S(2)}) async-start(), calls=%async_computation.2 | async-start | bytes 1114112 | tf_op jit(solution)/shard_map/all_gather | solution.py:20
  307.4 432.8 %copy-start.1 = (bf16[128,896]{1,0:T(8,128)(2,1)S(1)}, bf16[128,896]{1,0:T(8,128)(2,1)}, u32[]{:S(2)}) copy-start(bf16[128,896]{1,0:T(8,128)(2,1)} %param.6) | copy-start | bytes 688132
  307.4 444.5 %all-to-all-start = ((bf16[32,2,57344]{2,1,0:T(2,128)(2,1)}), bf16[32,2,57344]{2,1,0:T(2,128)(2,1)}, u32[]{:S(2)}, u32[]{:S(2)}) async-start(bf16[32,2,57344]{2,1,0:T(2,128)(2,1)} %reshape.33), calls=%async_computation.1 | async-start | bytes 14680064 | tf_op jit(solution)/shard_map/all_to_all | solution.py:36
  320.4 426.4 %copy-start = (bf16[128,4096]{1,0:T(8,128)(2,1)S(1)}, bf16[128,4096]{1,0:T(8,128)(2,1)}, u32[]{:S(2)}) copy-start(bf16[128,4096]{1,0:T(8,128)(2,1)} %all-gather.3.cloned.1.call-done) | copy-start | bytes 3145732
  320.4 419.8 %all-gather.5.cloned.1.call-start = ((), (), s32[]{:S(2)}) async-start(), calls=%async_computation.3 | async-start | bytes 7569408 | tf_op jit(solution)/shard_map/all_gather | solution.py:23
  321.0 513.6 %reduce-scatter.2.cloned.1.call-start = ((), (), s32[]{:S(2)}) async-start(), calls=%async_computation.4 | async-start | bytes 1114112 | tf_op jit(solution)/shard_map/reduce_scatter | solution.py:29
Sparse Core Ops, SparseCore 0:
  10.8 80.8 all-gather.2
  746.9 87.6 reduce-scatter.1
Sparse Core Ops, SparseCore 1:
  324.0 416.1 all-gather.4
where the time goes:
time: 845 us; the launch traced here: 842 us
  waiting for transfers between devices  544 us (64%)
  other arithmetic  164 us (19%)
  local copies, waits for them, and re-layouts  87.4 us (10%)
  matrix products  18 us (2%)
  between operations  15.5 us (2%)
  starting transfers between devices  13.4 us (2%)
    all_gather x1, waiting for transfers between devices, on_device(): weight_piece = lax.all_gather(weight, 'dp', axis=0, tiled=True)  419 us
    unnamed x1, other arithmetic  157 us
    all_gather x1, waiting for transfers between devices, on_device(): features_all = lax.all_gather(tokens, 'tensor', axis=1, tiled=True)  82.2 us
    unnamed x10, local copies, waits for them, and re-layouts  55.2 us
    reduce_scatter x1, waiting for transfers between devices, on_device(): lax.psum_scatter(input_term.astype(jnp.bfloat16), 'tensor', scatter_dimen...  41.6 us
    broadcast_in_dim x1, local copies, waits for them, and re-layouts, on_device(): local_grad[None]  32.2 us
  transfers between devices with their start and end apart: 4, of which 3 were waited for; matrix products, arithmetic and copies ran while one was open for 6% of the time, Pallas kernels for 0%

commit v1 on v0

v1 whole, which is shorter than its diff:
```python
import jax
import jax.numpy as jnp
from jax import lax
from jax.experimental.layout import Layout, with_layout_constraint
from jax.sharding import PartitionSpec as P

BLOCK = 512
RING = 4
GROUPS = 16


def dp_of(x, z, core):
    return ((x % RING) * RING + z % RING) * 2 + core


def dp_pairs(dz, flip):
    return [
        (dp_of(x, z + dz, core ^ flip), dp_of(x, z, core))
        for x in range(RING)
        for z in range(RING)
        for core in range(2)
    ]


def swap_pairs(flip):
    return [
        (
            dp_of(y, z, core ^ flip) * GROUPS + x * RING + low,
            dp_of(x, z, core) * GROUPS + y * RING + low,
        )
        for x in range(RING)
        for z in range(RING)
        for core in range(2)
        for y in range(RING)
        for low in range(RING)
    ]


def groups_x():
    return [[dp_of(x, z, core) for x in range(RING)] for z in range(RING) for core in range(2)]


def groups_y():
    return [[y * RING + low for y in range(RING)] for low in range(RING)]


def groups_low():
    return [[y * RING + low for low in range(RING)] for y in range(RING)]


def from_core(block):
    return lax.ppermute(block, "dp", dp_pairs(0, 1))


def from_z(block, shift):
    return lax.ppermute(block, "dp", dp_pairs(shift, 0))


def from_swap(block, flip):
    return lax.ppermute(block, ("dp", "tensor"), swap_pairs(flip))


def row_major(array):
    return with_layout_constraint(array, Layout(major_to_minor=tuple(range(array.ndim))))


def exchange(parts, axis, groups):
    parts = row_major(parts)
    return row_major(lax.all_to_all(parts, axis, 0, 0, axis_index_groups=groups, tiled=True))


def collect(block, axis, groups):
    return exchange(jnp.broadcast_to(block[None], (RING,) + block.shape), axis, groups)


def rolled(array, start):
    return lax.dynamic_slice_in_dim(jnp.concatenate([array, array], axis=0), start, array.shape[0], 0)


def total(parts):
    return jnp.sum(parts.astype(jnp.float32), axis=0)


def on_device(tokens, weight, cotangent, levels):
    token_rows, local_features = tokens.shape
    local_cols = weight.shape[1]
    half = local_features // 2
    dp_count = lax.axis_size("dp")
    dp = lax.axis_index("dp")
    tensor = lax.axis_index("tensor")
    core = dp % 2
    z_hi = (dp // 2) % RING
    wide = jnp.float32
    narrow = jnp.bfloat16

    col_start = tensor * local_cols
    column_ids = col_start + jnp.arange(local_cols, dtype=jnp.int32)
    block_ids = column_ids // BLOCK
    block_range = jnp.arange(levels.shape[0], dtype=jnp.int32)
    membership = (block_ids[None, :] == block_range[:, None]).astype(wide)
    level_vals = levels.astype(wide) / 8.0
    col_scale = jnp.sum(membership * level_vals[:, None], axis=0)

    scaled = (cotangent.astype(wide) * col_scale[None, :]).astype(narrow)
    tokens, scaled = lax.optimization_barrier((tokens, scaled))

    ahead = from_z(weight, 1)
    behind = from_z(weight, -1)
    mid = weight.shape[0] // 2
    far_top = from_z(ahead[:mid], 1)
    far_low = from_z(behind[mid:], -1)
    weight_line = jnp.concatenate([weight, ahead, far_top, far_low, behind], axis=0)

    keep = lax.dynamic_slice_in_dim(tokens, core * half, half, 1)
    give = lax.dynamic_slice_in_dim(tokens, (1 - core) * half, half, 1)
    pair = row_major(jnp.stack([from_swap(keep, 0), from_swap(give, 1)]))
    line = rolled(collect(pair, "tensor", groups_low()), z_hi).reshape(RING, 2 * token_rows, half)
    line = jnp.concatenate([line[i] for i in range(RING)], axis=1)
    brick = collect(line, "tensor", groups_y()).reshape(-1, RING * half)

    scaled_own = collect(scaled, "dp", groups_x())
    scaled_all = jnp.stack([scaled_own, from_core(scaled_own)], axis=1).reshape(-1, local_cols)

    grads = lax.dot_general(brick, scaled_all, (((0,), (0,)), ((), ())), preferred_element_type=wide)
    grads = grads.reshape(RING, 2, mid, local_cols)
    far = grads[2].astype(narrow)
    far, weight_line = lax.optimization_barrier((far, weight_line))
    top = from_z(far[0], -1).astype(wide)
    low = from_z(far[1], 1).astype(wide)
    up = jnp.stack([grads[1, 0] + top, grads[1, 1]]).astype(narrow)
    down = jnp.stack([grads[3, 0], grads[3, 1] + low]).astype(narrow)
    grad_sum = grads[0] + from_z(up, -1).astype(wide) + from_z(down, 1).astype(wide)
    grad_factor = 1.0 / jnp.sqrt(jnp.float32(token_rows * dp_count))
    weight_grad = grad_sum.reshape(-1, local_cols) * grad_factor

    term = lax.dot_general(scaled_all, weight_line, (((1,), (1,)), ((), ())), preferred_element_type=wide)
    term = row_major(term.astype(narrow)).reshape(RING, 2 * token_rows, RING * half)
    term = total(exchange(term, "tensor", groups_y()))
    term = term.astype(narrow)
    term = jnp.stack([term[:, i * half:(i + 1) * half] for i in range(RING)])
    term = rolled(term, (RING - z_hi) % RING)
    term = total(exchange(term, "tensor", groups_low())).astype(narrow)
    mine = from_swap(term[:token_rows], 0)
    other = from_swap(term[token_rows:], 1)
    input_grad = jnp.concatenate(
        [jnp.where(core == 0, mine, other), jnp.where(core == 0, other, mine)], axis=1
    )

    share = jnp.dot(brick, weight_line, preferred_element_type=wide)
    share = share.reshape(RING, 2, token_rows, local_cols)
    share = share[:, 0] + from_core(share[:, 1].astype(narrow)).astype(wide)
    running = total(exchange(share.astype(narrow), "dp", groups_x()))
    output = (running * col_scale[None, :]).astype(narrow)
    return (output, input_grad, weight_grad)


def solution(mesh):
    placed = (P("dp", "tensor"), P("dp", "tensor"), P("dp", "tensor"), P())
    return jax.shard_map(
        on_device,
        mesh=mesh,
        in_specs=placed,
        out_specs=(P("dp", "tensor"), P("dp", "tensor"), P("dp", "tensor")),
        check_vma=False,
    )
```

time: 845 us -> 171 us (0.20)
  the two profiles are of different devices: /device:TPU:6 before, /device:TPU:123 now
where the time goes in v1:
time: 171 us; the launch traced here: 170 us
  starting transfers between devices  90.9 us (53%)
  waiting for transfers between devices  49.6 us (29%)
  other arithmetic  11.6 us (7%)
  local copies, waits for them, and re-layouts  10 us (6%)
  matrix products  6.44 us (4%)
    ppermute x8, waiting for transfers between devices, from_z(): return lax.ppermute(block, 'dp', dp_pairs(shift, 0))  41.2 us
    ppermute x8, starting transfers between devices, from_z(): return lax.ppermute(block, 'dp', dp_pairs(shift, 0))  35.5 us
    all_to_all x6, starting transfers between devices, exchange(): lax.all_to_all(parts, axis, 0, 0, axis_index_groups=groups, tiled=True)  28.6 us
    ppermute x4, starting transfers between devices, from_swap(): return lax.ppermute(block, ('dp', 'tensor'), swap_pairs(flip))  20.4 us
    ppermute x4, waiting for transfers between devices, from_swap(): return lax.ppermute(block, ('dp', 'tensor'), swap_pairs(flip))  8.42 us
    ppermute x2, starting transfers between devices, from_core(): return lax.ppermute(block, 'dp', dp_pairs(0, 1))  6.35 us
    unnamed x23, local copies, waits for them, and re-layouts  3.84 us
  transfers between devices with their start and end apart: 20, of which 9 were waited for; matrix products, arithmetic and copies ran while one was open for 9% of the time, Pallas kernels for 0%

profile of v1, /device:TPU:123, one launch (start us, length us, event | category | flops | bytes accessed | tf_op | source)
XLA Modules:
  0.0 169.7 jit_solution(9069237767433887500)
XLA Ops:
  0.6 0.7 convert_multiply_fusion
  1.3 0.1 select_reduce_fusion
  1.4 1.0 multiply_convert_fusion.1
  2.4 1.0 broadcast_in_dim.8
  3.4 4.3 %all-to-all-start.2 = ((bf16[4,128,896]{2,1,0:T(8,128)(2,1)}), bf16[4,128,896]{2,1,0:T(8,128)(2,1)S(1)}, u32[]{:S(2)}, u32[]{:S(2)}) async-start(bf16[4,128,896]{2,1,0:T(8,128)(2,1)} %broadcast_in_dim.8), calls=%async_computation.2 | async-start | bytes 1835008 | tf_op jit(solution)/shard_map/all_to_all | solution.py:69
  7.7 4.4 %collective-permute-start = (bf16[128,128]{1,0:T(8,128)(2,1)S(1)}, bf16[128,128]{1,0:T(8,128)(2,1)S(1)}, u32[]{:S(2)}, u32[]{:S(2)}) collective-permute-start(bf16[128,128]{1,0:T(8,128)(2,1)S(1)} %get-tuple-element.25), channel_id=1, source_target_pairs={{0,0},{1,1},{2,2},{3,3},{128,4},{129,5},{130,6},{131,7},{256,8},{2... | collective-permute-start | bytes 98312 | tf_op jit(solution)/shard_map/ppermute | solution.py:60
  12.1 6.2 %collective-permute-start.1 = (bf16[128,128]{1,0:T(8,128)(2,1)S(1)}, bf16[128,128]{1,0:T(8,128)(2,1)S(1)}, u32[]{:S(2)}, u32[]{:S(2)}) collective-permute-start(bf16[128,128]{1,0:T(8,128)(2,1)S(1)} %get-tuple-element.26), channel_id=1, source_target_pairs={{16,0},{17,1},{18,2},{19,3},{144,4},{145,5},{146,6},{147,7},{272,8... | collective-permute-start | bytes 98312 | tf_op jit(solution)/shard_map/ppermute | solution.py:60
  18.3 2.3 %collective-permute-done = bf16[128,128]{1,0:T(8,128)(2,1)S(1)} collective-permute-done((bf16[128,128]{1,0:T(8,128)(2,1)S(1)}, bf16[128,128]{1,0:T(8,128)(2,1)S(1)}, u32[]{:S(2)}, u32[]{:S(2)}) %collective-permute-start) | collective-permute-done | bytes 32800 | tf_op jit(solution)/shard_map/ppermute | solution.py:60
  20.6 2.1 %collective-permute-done.1 = bf16[128,128]{1,0:T(8,128)(2,1)S(1)} collective-permute-done((bf16[128,128]{1,0:T(8,128)(2,1)S(1)}, bf16[128,128]{1,0:T(8,128)(2,1)S(1)}, u32[]{:S(2)}, u32[]{:S(2)}) %collective-permute-start.1) | collective-permute-done | bytes 32800 | tf_op jit(solution)/shard_map/ppermute | solution.py:60
  22.8 0.0 all-to-all-done.2
  22.8 0.7 broadcast_in_dim.6
  23.5 4.5 %all-to-all-start = ((bf16[4,2,128,128]{3,2,1,0:T(8,128)(2,1)}), bf16[4,2,128,128]{3,2,1,0:T(8,128)(2,1)S(1)}, u32[]{:S(2)}, u32[]{:S(2)}) async-start(bf16[4,2,128,128]{3,2,1,0:T(8,128)(2,1)} %broadcast_in_dim.6), calls=%async_computation | async-start | bytes 524288 | tf_op jit(solution)/shard_map/all_to_all | solution.py:69
  28.1 10.2 %collective-permute-start.3 = (bf16[128,896]{1,0:T(8,128)(2,1)}, bf16[128,896]{1,0:T(8,128)(2,1)S(1)}, u32[]{:S(2)}, u32[]{:S(2)}) collective-permute-start(bf16[128,896]{1,0:T(8,128)(2,1)} %param.5), channel_id=1, source_target_pairs={{32,0},{48,16},{64,32},{80,48},{96,64},{112,80},{0,96},{16,112},{1... | collective-permute-start | bytes 688136 | tf_op jit(solution)/shard_map/ppermute | solution.py:56
  38.3 1.9 %collective-permute-start.5 = (bf16[128,896]{1,0:T(8,128)(2,1)}, bf16[128,896]{1,0:T(8,128)(2,1)S(1)}, u32[]{:S(2)}, u32[]{:S(2)}) collective-permute-start(bf16[128,896]{1,0:T(8,128)(2,1)} %param.5), channel_id=1, source_target_pairs={{96,0},{112,16},{0,32},{16,48},{32,64},{48,80},{64,96},{80,112},{2... | collective-permute-start | bytes 688136 | tf_op jit(solution)/shard_map/ppermute | solution.py:56
  40.2 2.9 %collective-permute-start.2 = (bf16[4,128,896]{2,1,0:T(8,128)(2,1)S(1)}, bf16[4,128,896]{2,1,0:T(8,128)(2,1)S(1)}, u32[]{:S(2)}, u32[]{:S(2)}) collective-permute-start(bf16[4,128,896]{2,1,0:T(8,128)(2,1)S(1)} %all-to-all-done.2), channel_id=1, source_target_pairs={{16,0},{0,16},{48,32},{32,48},{80,64},{64,80},{112,96},{96,112},{1... | collective-permute-start | bytes 2752520 | tf_op jit(solution)/shard_map/ppermute | solution.py:52
  43.2 0.0 all-to-all-done
  43.2 0.1 fusion.6
  43.4 1.1 broadcast_in_dim.7
  44.4 4.2 %all-to-all-start.1 = ((bf16[4,256,512]{2,1,0:T(8,128)(2,1)}), bf16[4,256,512]{2,1,0:T(8,128)(2,1)S(1)}, u32[]{:S(2)}, u32[]{:S(2)}) async-start(bf16[4,256,512]{2,1,0:T(8,128)(2,1)} %broadcast_in_dim.7), calls=%async_computation.1 | async-start | bytes 2097152 | tf_op jit(solution)/shard_map/all_to_all | solution.py:69
  48.6 1.0 constant_dynamic-update-slice_fusion.4
  49.6 4.9 %collective-permute-done.3 = bf16[128,896]{1,0:T(8,128)(2,1)S(1)} collective-permute-done((bf16[128,896]{1,0:T(8,128)(2,1)}, bf16[128,896]{1,0:T(8,128)(2,1)S(1)}, u32[]{:S(2)}, u32[]{:S(2)}) %collective-permute-start.3) | collective-permute-done | bytes 229408 | tf_op jit(solution)/shard_map/ppermute | solution.py:56
  54.5 2.9 %collective-permute-start.4 = (bf16[64,896]{1,0:T(8,128)(2,1)S(1)}, bf16[64,896]{1,0:T(8,128)(2,1)S(1)}, u32[]{:S(2)}, u32[]{:S(2)}) collective-permute-start(bf16[64,896]{1,0:T(8,128)(2,1)S(1)} %slice.103), channel_id=1, source_target_pairs={{32,0},{48,16},{64,32},{80,48},{96,64},{112,80},{0,96},{16,112},{1... | collective-permute-start | bytes 344072 | tf_op jit(solution)/shard_map/ppermute | solution.py:56
  57.4 8.9 %collective-permute-done.5 = bf16[128,896]{1,0:T(8,128)(2,1)S(1)} collective-permute-done((bf16[128,896]{1,0:T(8,128)(2,1)}, bf16[128,896]{1,0:T(8,128)(2,1)S(1)}, u32[]{:S(2)}, u32[]{:S(2)}) %collective-permute-start.5) | collective-permute-done | bytes 229408 | tf_op jit(solution)/shard_map/ppermute | solution.py:56
  66.3 1.9 %collective-permute-start.6 = (bf16[64,896]{1,0:T(8,128)(2,1)S(1)}, bf16[64,896]{1,0:T(8,128)(2,1)S(1)}, u32[]{:S(2)}, u32[]{:S(2)}) collective-permute-start(bf16[64,896]{1,0:T(8,128)(2,1)S(1)} %slice.104), channel_id=1, source_target_pairs={{96,0},{112,16},{0,32},{16,48},{32,64},{48,80},{64,96},{80,112},{2... | collective-permute-start | bytes 344072 | tf_op jit(solution)/shard_map/ppermute | solution.py:56
  68.3 2.4 %collective-permute-done.4 = bf16[64,896]{1,0:T(8,128)(2,1)S(1)} collective-permute-done((bf16[64,896]{1,0:T(8,128)(2,1)S(1)}, bf16[64,896]{1,0:T(8,128)(2,1)S(1)}, u32[]{:S(2)}, u32[]{:S(2)}) %collective-permute-start.4) | collective-permute-done | bytes 114720 | tf_op jit(solution)/shard_map/ppermute | solution.py:56
  70.8 9.2 %collective-permute-done.6 = bf16[64,896]{1,0:T(8,128)(2,1)S(1)} collective-permute-done((bf16[64,896]{1,0:T(8,128)(2,1)S(1)}, bf16[64,896]{1,0:T(8,128)(2,1)S(1)}, u32[]{:S(2)}, u32[]{:S(2)}) %collective-permute-start.6) | collective-permute-done | bytes 114720 | tf_op jit(solution)/shard_map/ppermute | solution.py:56
  80.1 0.0 collective-permute-done.2
  80.1 0.9 copy-done.2
  81.0 0.2 pad_maximum_fusion
  81.2 1.4 copy.12
  82.6 2.9 %fusion.26 = f32[512,896]{1,0:T(8,128)S(1)} fusion(bf16[1024,512]{1,0:T(8,128)(2,1)S(1)} %bitcast.85, bf16[1024,896]{1,0:T(8,128)(2,1)} %bitcast.87), kind=kOutput, calls=%fused_computation.71 | convolution fusion | flops 939524096 | bytes 4718592 | tf_op jit(solution)/shard_map/dot_general | solution.py:124
  85.5 2.3 %convolution_convert_fusion = bf16[1024,512]{1,0:T(8,128)(2,1)} fusion(bf16[1024,896]{1,0:T(8,128)(2,1)S(1)} %bitcast.88, bf16[512,896]{1,0:T(8,128)(2,1)S(1)} %copy-done.3), kind=kOutput, calls=%fused_computation.6 | convolution fusion | flops 940048384 | bytes 3801088 | tf_op jit(solution)/shard_map/dot_general | solution.py:136
  87.9 4.2 %all-to-all-start.4 = ((bf16[4,256,512]{2,1,0:T(8,128)(2,1)}), bf16[4,256,512]{2,1,0:T(8,128)(2,1)}, u32[]{:S(2)}, u32[]{:S(2)}) async-start(bf16[4,256,512]{2,1,0:T(8,128)(2,1)} %bitcast.91), calls=%async_computation.4 | async-start | bytes 2097152 | tf_op jit(solution)/shard_map/all_to_all | solution.py:69
  92.1 4.0 %collective-permute-start.10 = (bf16[64,896]{1,0:T(8,128)(2,1)S(1)}, bf16[64,896]{1,0:T(8,128)(2,1)S(1)}, u32[]{:S(2)}, u32[]{:S(2)}) collective-permute-start(bf16[64,896]{1,0:T(8,128)(2,1)S(1)} %get-tuple-element.19), channel_id=1, source_target_pairs={{96,0},{112,16},{0,32},{16,48},{32,64},{48,80},{64,96},{80,112},{2... | collective-permute-start | bytes 344072 | tf_op jit(solution)/shard_map/ppermute | solution.py:56
  96.1 5.4 %collective-permute-start.12 = (bf16[64,896]{1,0:T(8,128)(2,1)S(1)}, bf16[64,896]{1,0:T(8,128)(2,1)}, u32[]{:S(2)}, u32[]{:S(2)}) collective-permute-start(bf16[64,896]{1,0:T(8,128)(2,1)S(1)} %get-tuple-element.20), channel_id=1, source_target_pairs={{32,0},{48,16},{64,32},{80,48},{96,64},{112,80},{0,96},{16,112},{1... | collective-permute-start | bytes 344072 | tf_op jit(solution)/shard_map/ppermute | solution.py:56
  101.5 0.1 convert.27
  101.6 1.3 fusion.2
  102.9 1.8 %copy-done = f32[4,2,128,896]{3,2,0,1:T(8,128)} copy-done((f32[4,2,128,896]{3,2,0,1:T(8,128)}, f32[4,2,128,896]{3,2,0,1:T(8,128)S(1)}, u32[]{:S(2)}) %copy-start) | copy-done | bytes 3670040
  104.7 1.0 fusion.4
  105.7 3.4 %collective-permute-start.7 = (bf16[4,128,896]{2,1,0:T(8,128)(2,1)}, bf16[4,128,896]{2,1,0:T(8,128)(2,1)}, u32[]{:S(2)}, u32[]{:S(2)}) collective-permute-start(bf16[4,128,896]{2,1,0:T(8,128)(2,1)} %fusion.4), channel_id=1, source_target_pairs={{16,0},{0,16},{48,32},{32,48},{80,64},{64,80},{112,96},{96,112},{1... | collective-permute-start | bytes 2752520 | tf_op jit(solution)/shard_map/ppermute | solution.py:52
  109.2 0.0 all-to-all-done.4
  109.2 1.5 reduce_sum.44
  110.8 0.7 constant_dynamic-slice_fusion
  111.5 6.3 %all-to-all-start.5 = ((bf16[4,256,128]{2,1,0:T(8,128)(2,1)}), bf16[4,256,128]{2,1,0:T(8,128)(2,1)S(1)}, u32[]{:S(2)}, u32[]{:S(2)}) async-start(bf16[4,256,128]{2,1,0:T(8,128)(2,1)} %constant_dynamic-slice_fusion), calls=%async_computation.5 | async-start | bytes 524288 | tf_op jit(solution)/shard_map/all_to_all | solution.py:69
  117.8 0.0 collective-permute-done.10
  117.8 0.0 collective-permute-done.12
  117.8 0.9 fusion.11
  118.8 4.7 %collective-permute-start.13 = (bf16[2,64,896]{2,1,0:T(8,128)(2,1)S(1)}, bf16[2,64,896]{2,1,0:T(8,128)(2,1)}, u32[]{:S(2)}, u32[]{:S(2)}) collective-permute-start(bf16[2,64,896]{2,1,0:T(8,128)(2,1)S(1)} %pad_maximum_fusion.3), channel_id=1, source_target_pairs={{32,0},{48,16},{64,32},{80,48},{96,64},{112,80},{0,96},{16,112},{1... | collective-permute-start | bytes 688136 | tf_op jit(solution)/shard_map/ppermute | solution.py:56
  123.5 0.7 pad_maximum_fusion.2
  124.2 4.5 %collective-permute-start.11 = (bf16[2,64,896]{2,1,0:T(8,128)(2,1)}, bf16[2,64,896]{2,1,0:T(8,128)(2,1)}, u32[]{:S(2)}, u32[]{:S(2)}) collective-permute-start(bf16[2,64,896]{2,1,0:T(8,128)(2,1)} %pad_maximum_fusion.2), channel_id=1, source_target_pairs={{96,0},{112,16},{0,32},{16,48},{32,64},{48,80},{64,96},{80,112},{2... | collective-permute-start | bytes 688136 | tf_op jit(solution)/shard_map/ppermute | solution.py:56
  128.7 0.0 collective-permute-done.7
  128.7 2.8 %fusion.1 = bf16[4,128,896]{2,1,0:T(8,128)(2,1)} fusion(f32[4,2,128,896]{3,2,0,1:T(8,128)} %copy-done, bf16[4,128,896]{2,1,0:T(8,128)(2,1)} %collective-permute-done.7), kind=kLoop, calls=%fused_computation.3 | loop fusion | flops 1376256 | bytes 3670016 | tf_op jit(solution)/shard_map/convert_element_type | solution.py:152
  131.6 0.0 all-to-all-done.5
  131.6 5.1 %all-to-all-start.3 = ((bf16[4,128,896]{2,1,0:T(8,128)(2,1)}), bf16[4,128,896]{2,1,0:T(8,128)(2,1)S(1)}, u32[]{:S(2)}, u32[]{:S(2)}) async-start(bf16[4,128,896]{2,1,0:T(8,128)(2,1)} %fusion.1), calls=%async_computation.3 | async-start | bytes 1835008 | tf_op jit(solution)/shard_map/all_to_all | solution.py:69
  136.7 2.7 %collective-permute-done.13 = bf16[2,64,896]{2,1,0:T(8,128)(2,1)} collective-permute-done((bf16[2,64,896]{2,1,0:T(8,128)(2,1)S(1)}, bf16[2,64,896]{2,1,0:T(8,128)(2,1)}, u32[]{:S(2)}, u32[]{:S(2)}) %collective-permute-start.13) | collective-permute-done | bytes 229408 | tf_op jit(solution)/shard_map/ppermute | solution.py:56
  139.5 12.9 %collective-permute-done.11 = bf16[2,64,896]{2,1,0:T(8,128)(2,1)} collective-permute-done((bf16[2,64,896]{2,1,0:T(8,128)(2,1)}, bf16[2,64,896]{2,1,0:T(8,128)(2,1)}, u32[]{:S(2)}, u32[]{:S(2)}) %collective-permute-start.11) | collective-permute-done | bytes 229408 | tf_op jit(solution)/shard_map/ppermute | solution.py:56
  152.4 1.9 %add_multiply_fusion = f32[2,64,896]{2,1,0:T(8,128)} fusion(bf16[2,64,896]{2,1,0:T(8,128)(2,1)} %collective-permute-done.13, f32[2,64,896]{2,1,0:T(8,128)S(1)} %bitcast.90, bf16[2,64,896]{2,1,0:T(8,128)(2,1)} %collective-permute-done.11), kind=kLoop, calls=%fused_computation.14 | loop fusion | flops 573440 | bytes 1376256 | tf_op jit(solution)/shard_map/mul | solution.py:134
  154.4 5.0 %collective-permute-start.8 = (bf16[128,128]{1,0:T(8,128)(2,1)S(1)}, bf16[128,128]{1,0:T(8,128)(2,1)S(1)}, u32[]{:S(2)}, u32[]{:S(2)}) collective-permute-start(bf16[128,128]{1,0:T(8,128)(2,1)S(1)} %get-tuple-element.23), channel_id=1, source_target_pairs={{0,0},{1,1},{2,2},{3,3},{128,4},{129,5},{130,6},{131,7},{256,8},{2... | collective-permute-start | bytes 98312 | tf_op jit(solution)/shard_map/ppermute | solution.py:60
  159.3 4.9 %collective-permute-start.9 = (bf16[128,128]{1,0:T(8,128)(2,1)S(1)}, bf16[128,128]{1,0:T(8,128)(2,1)S(1)}, u32[]{:S(2)}, u32[]{:S(2)}) collective-permute-start(bf16[128,128]{1,0:T(8,128)(2,1)S(1)} %get-tuple-element.24), channel_id=1, source_target_pairs={{16,0},{17,1},{18,2},{19,3},{144,4},{145,5},{146,6},{147,7},{272,8... | collective-permute-start | bytes 98312 | tf_op jit(solution)/shard_map/ppermute | solution.py:60
  164.2 0.1 convert_reduce_fusion
  164.4 0.7 multiply_convert_fusion
  165.1 0.0 collective-permute-done.8
  165.1 4.0 %collective-permute-done.9 = bf16[128,128]{1,0:T(8,128)(2,1)S(1)} collective-permute-done((bf16[128,128]{1,0:T(8,128)(2,1)S(1)}, bf16[128,128]{1,0:T(8,128)(2,1)S(1)}, u32[]{:S(2)}, u32[]{:S(2)}) %collective-permute-start.9) | collective-permute-done | bytes 32800 | tf_op jit(solution)/shard_map/ppermute | solution.py:60
  169.1 0.6 pad_maximum_fusion.5
  (39 shorter events, 0.5 us)
Async XLA Ops:
  0.6 7.1 %copy-start.5 = (bf16[128,256]{1,0:T(8,128)(2,1)S(1)}, bf16[128,256]{1,0:T(8,128)(2,1)}, u32[]{:S(2)}) copy-start(bf16[128,256]{1,0:T(8,128)(2,1)} %param.4) | copy-start | bytes 196612
  3.4 19.3 %all-to-all-start.2 = ((bf16[4,128,896]{2,1,0:T(8,128)(2,1)}), bf16[4,128,896]{2,1,0:T(8,128)(2,1)S(1)}, u32[]{:S(2)}, u32[]{:S(2)}) async-start(bf16[4,128,896]{2,1,0:T(8,128)(2,1)} %broadcast_in_dim.8), calls=%async_computation.2 | async-start | bytes 1835008 | tf_op jit(solution)/shard_map/all_to_all | solution.py:69
  7.7 12.9 %collective-permute-start = (bf16[128,128]{1,0:T(8,128)(2,1)S(1)}, bf16[128,128]{1,0:T(8,128)(2,1)S(1)}, u32[]{:S(2)}, u32[]{:S(2)}) collective-permute-start(bf16[128,128]{1,0:T(8,128)(2,1)S(1)} %get-tuple-element.25), channel_id=1, source_target_pairs={{0,0},{1,1},{2,2},{3,3},{128,4},{129,5},{130,6},{131,7},{256,8},{2... | collective-permute-start | bytes 98312 | tf_op jit(solution)/shard_map/ppermute | solution.py:60
  12.1 10.7 %collective-permute-start.1 = (bf16[128,128]{1,0:T(8,128)(2,1)S(1)}, bf16[128,128]{1,0:T(8,128)(2,1)S(1)}, u32[]{:S(2)}, u32[]{:S(2)}) collective-permute-start(bf16[128,128]{1,0:T(8,128)(2,1)S(1)} %get-tuple-element.26), channel_id=1, source_target_pairs={{16,0},{17,1},{18,2},{19,3},{144,4},{145,5},{146,6},{147,7},{272,8... | collective-permute-start | bytes 98312 | tf_op jit(solution)/shard_map/ppermute | solution.py:60
  23.5 19.6 %all-to-all-start = ((bf16[4,2,128,128]{3,2,1,0:T(8,128)(2,1)}), bf16[4,2,128,128]{3,2,1,0:T(8,128)(2,1)S(1)}, u32[]{:S(2)}, u32[]{:S(2)}) async-start(bf16[4,2,128,128]{3,2,1,0:T(8,128)(2,1)} %broadcast_in_dim.6), calls=%async_computation | async-start | bytes 524288 | tf_op jit(solution)/shard_map/all_to_all | solution.py:69
  28.1 26.4 %collective-permute-start.3 = (bf16[128,896]{1,0:T(8,128)(2,1)}, bf16[128,896]{1,0:T(8,128)(2,1)S(1)}, u32[]{:S(2)}, u32[]{:S(2)}) collective-permute-start(bf16[128,896]{1,0:T(8,128)(2,1)} %param.5), channel_id=1, source_target_pairs={{32,0},{48,16},{64,32},{80,48},{96,64},{112,80},{0,96},{16,112},{1... | collective-permute-start | bytes 688136 | tf_op jit(solution)/shard_map/ppermute | solution.py:56
  38.3 28.1 %collective-permute-start.5 = (bf16[128,896]{1,0:T(8,128)(2,1)}, bf16[128,896]{1,0:T(8,128)(2,1)S(1)}, u32[]{:S(2)}, u32[]{:S(2)}) collective-permute-start(bf16[128,896]{1,0:T(8,128)(2,1)} %param.5), channel_id=1, source_target_pairs={{96,0},{112,16},{0,32},{16,48},{32,64},{48,80},{64,96},{80,112},{2... | collective-permute-start | bytes 688136 | tf_op jit(solution)/shard_map/ppermute | solution.py:56
  40.2 39.8 %collective-permute-start.2 = (bf16[4,128,896]{2,1,0:T(8,128)(2,1)S(1)}, bf16[4,128,896]{2,1,0:T(8,128)(2,1)S(1)}, u32[]{:S(2)}, u32[]{:S(2)}) collective-permute-start(bf16[4,128,896]{2,1,0:T(8,128)(2,1)S(1)} %all-to-all-done.2), channel_id=1, source_target_pairs={{16,0},{0,16},{48,32},{32,48},{80,64},{64,80},{112,96},{96,112},{1... | collective-permute-start | bytes 2752520 | tf_op jit(solution)/shard_map/ppermute | solution.py:52
  44.4 38.1 %all-to-all-start.1 = ((bf16[4,256,512]{2,1,0:T(8,128)(2,1)}), bf16[4,256,512]{2,1,0:T(8,128)(2,1)S(1)}, u32[]{:S(2)}, u32[]{:S(2)}) async-start(bf16[4,256,512]{2,1,0:T(8,128)(2,1)} %broadcast_in_dim.7), calls=%async_computation.1 | async-start | bytes 2097152 | tf_op jit(solution)/shard_map/all_to_all | solution.py:69
  54.5 16.3 %collective-permute-start.4 = (bf16[64,896]{1,0:T(8,128)(2,1)S(1)}, bf16[64,896]{1,0:T(8,128)(2,1)S(1)}, u32[]{:S(2)}, u32[]{:S(2)}) collective-permute-start(bf16[64,896]{1,0:T(8,128)(2,1)S(1)} %slice.103), channel_id=1, source_target_pairs={{32,0},{48,16},{64,32},{80,48},{96,64},{112,80},{0,96},{16,112},{1... | collective-permute-start | bytes 344072 | tf_op jit(solution)/shard_map/ppermute | solution.py:56
  66.3 13.7 %collective-permute-start.6 = (bf16[64,896]{1,0:T(8,128)(2,1)S(1)}, bf16[64,896]{1,0:T(8,128)(2,1)S(1)}, u32[]{:S(2)}, u32[]{:S(2)}) collective-permute-start(bf16[64,896]{1,0:T(8,128)(2,1)S(1)} %slice.104), channel_id=1, source_target_pairs={{96,0},{112,16},{0,32},{16,48},{32,64},{48,80},{64,96},{80,112},{2... | collective-permute-start | bytes 344072 | tf_op jit(solution)/shard_map/ppermute | solution.py:56
  80.0 0.9 copy-start.2
  82.6 3.0 %copy-start.1 = (bf16[4,2,128,896]{3,2,1,0:T(8,128)(2,1)S(1)}, bf16[4,2,128,896]{3,2,1,0:T(8,128)(2,1)}, u32[]{:S(2)}) copy-start(bf16[4,2,128,896]{3,2,1,0:T(8,128)(2,1)} %copy.12) | copy-start | bytes 5505028
  82.6 3.0 %copy-start.3 = (bf16[512,896]{1,0:T(8,128)(2,1)S(1)}, bf16[512,896]{1,0:T(8,128)(2,1)}, u32[]{:S(2)}) copy-start(bf16[512,896]{1,0:T(8,128)(2,1)} %copy-done.2) | copy-start | bytes 2752516
  87.9 21.3 %all-to-all-start.4 = ((bf16[4,256,512]{2,1,0:T(8,128)(2,1)}), bf16[4,256,512]{2,1,0:T(8,128)(2,1)}, u32[]{:S(2)}, u32[]{:S(2)}) async-start(bf16[4,256,512]{2,1,0:T(8,128)(2,1)} %bitcast.91), calls=%async_computation.4 | async-start | bytes 2097152 | tf_op jit(solution)/shard_map/all_to_all | solution.py:69
  92.1 9.5 %copy-start.4 = (bf16[512,896]{1,0:T(8,128)(2,1)S(1)}, bf16[512,896]{1,0:T(8,128)(2,1)}, u32[]{:S(2)}) copy-start(bf16[512,896]{1,0:T(8,128)(2,1)} %copy-done.2) | copy-start | bytes 2752516
  92.1 25.7 %collective-permute-start.10 = (bf16[64,896]{1,0:T(8,128)(2,1)S(1)}, bf16[64,896]{1,0:T(8,128)(2,1)S(1)}, u32[]{:S(2)}, u32[]{:S(2)}) collective-permute-start(bf16[64,896]{1,0:T(8,128)(2,1)S(1)} %get-tuple-element.19), channel_id=1, source_target_pairs={{96,0},{112,16},{0,32},{16,48},{32,64},{48,80},{64,96},{80,112},{2... | collective-permute-start | bytes 344072 | tf_op jit(solution)/shard_map/ppermute | solution.py:56
  96.1 21.7 %collective-permute-start.12 = (bf16[64,896]{1,0:T(8,128)(2,1)S(1)}, bf16[64,896]{1,0:T(8,128)(2,1)}, u32[]{:S(2)}, u32[]{:S(2)}) collective-permute-start(bf16[64,896]{1,0:T(8,128)(2,1)S(1)} %get-tuple-element.20), channel_id=1, source_target_pairs={{32,0},{48,16},{64,32},{80,48},{96,64},{112,80},{0,96},{16,112},{1... | collective-permute-start | bytes 344072 | tf_op jit(solution)/shard_map/ppermute | solution.py:56
  102.9 1.8 %copy-start = (f32[4,2,128,896]{3,2,0,1:T(8,128)}, f32[4,2,128,896]{3,2,0,1:T(8,128)S(1)}, u32[]{:S(2)}) copy-start(f32[4,2,128,896]{3,2,0,1:T(8,128)S(1)} %fusion.2) | copy-start | bytes 11010052
  105.7 23.0 %collective-permute-start.7 = (bf16[4,128,896]{2,1,0:T(8,128)(2,1)}, bf16[4,128,896]{2,1,0:T(8,128)(2,1)}, u32[]{:S(2)}, u32[]{:S(2)}) collective-permute-start(bf16[4,128,896]{2,1,0:T(8,128)(2,1)} %fusion.4), channel_id=1, source_target_pairs={{16,0},{0,16},{48,32},{32,48},{80,64},{64,80},{112,96},{96,112},{1... | collective-permute-start | bytes 2752520 | tf_op jit(solution)/shard_map/ppermute | solution.py:52
  111.5 20.0 %all-to-all-start.5 = ((bf16[4,256,128]{2,1,0:T(8,128)(2,1)}), bf16[4,256,128]{2,1,0:T(8,128)(2,1)S(1)}, u32[]{:S(2)}, u32[]{:S(2)}) async-start(bf16[4,256,128]{2,1,0:T(8,128)(2,1)} %constant_dynamic-slice_fusion), calls=%async_computation.5 | async-start | bytes 524288 | tf_op jit(solution)/shard_map/all_to_all | solution.py:69
  118.8 20.6 %collective-permute-start.13 = (bf16[2,64,896]{2,1,0:T(8,128)(2,1)S(1)}, bf16[2,64,896]{2,1,0:T(8,128)(2,1)}, u32[]{:S(2)}, u32[]{:S(2)}) collective-permute-start(bf16[2,64,896]{2,1,0:T(8,128)(2,1)S(1)} %pad_maximum_fusion.3), channel_id=1, source_target_pairs={{32,0},{48,16},{64,32},{80,48},{96,64},{112,80},{0,96},{16,112},{1... | collective-permute-start | bytes 688136 | tf_op jit(solution)/shard_map/ppermute | solution.py:56
  124.2 28.1 %collective-permute-start.11 = (bf16[2,64,896]{2,1,0:T(8,128)(2,1)}, bf16[2,64,896]{2,1,0:T(8,128)(2,1)}, u32[]{:S(2)}, u32[]{:S(2)}) collective-permute-start(bf16[2,64,896]{2,1,0:T(8,128)(2,1)} %pad_maximum_fusion.2), channel_id=1, source_target_pairs={{96,0},{112,16},{0,32},{16,48},{32,64},{48,80},{64,96},{80,112},{2... | collective-permute-start | bytes 688136 | tf_op jit(solution)/shard_map/ppermute | solution.py:56
  131.6 32.7 %all-to-all-start.3 = ((bf16[4,128,896]{2,1,0:T(8,128)(2,1)}), bf16[4,128,896]{2,1,0:T(8,128)(2,1)S(1)}, u32[]{:S(2)}, u32[]{:S(2)}) async-start(bf16[4,128,896]{2,1,0:T(8,128)(2,1)} %fusion.1), calls=%async_computation.3 | async-start | bytes 1835008 | tf_op jit(solution)/shard_map/all_to_all | solution.py:69
  154.4 10.7 %collective-permute-start.8 = (bf16[128,128]{1,0:T(8,128)(2,1)S(1)}, bf16[128,128]{1,0:T(8,128)(2,1)S(1)}, u32[]{:S(2)}, u32[]{:S(2)}) collective-permute-start(bf16[128,128]{1,0:T(8,128)(2,1)S(1)} %get-tuple-element.23), channel_id=1, source_target_pairs={{0,0},{1,1},{2,2},{3,3},{128,4},{129,5},{130,6},{131,7},{256,8},{2... | collective-permute-start | bytes 98312 | tf_op jit(solution)/shard_map/ppermute | solution.py:60
  159.3 9.7 %collective-permute-start.9 = (bf16[128,128]{1,0:T(8,128)(2,1)S(1)}, bf16[128,128]{1,0:T(8,128)(2,1)S(1)}, u32[]{:S(2)}, u32[]{:S(2)}) collective-permute-start(bf16[128,128]{1,0:T(8,128)(2,1)S(1)} %get-tuple-element.24), channel_id=1, source_target_pairs={{16,0},{17,1},{18,2},{19,3},{144,4},{145,5},{146,6},{147,7},{272,8... | collective-permute-start | bytes 98312 | tf_op jit(solution)/shard_map/ppermute | solution.py:60
